TPU v7x, 32 devices: a whole 2x2x4 slice. The times are simulated.
32 devices in a mesh: rows: 8 (over z, x), cols: 4 (over y, core).
Axes of the slice: x: 2, y: 2, z: 4, core: 2. Of those that a mesh axis runs over, the one named last changes fastest.
Arguments:
- column_lists: int32 [32, 13], replicated, may hold values from -1 to 31, as said below
- block_values: bfloat16 [32, 13, 128, 128], P('rows'), as said below
Outputs:
- purified: bfloat16 [32, 13, 128, 128], P('rows', None, None, 'cols')
Inputs may be any that keep to these rules, and one draw needn't show every extreme that they name: `column_lists`: slot (13 - 1) // 2 of row i holds i. Slot s of row i holds -1 or a row j, and then slot 12 - s of row j holds i. There is an ordering of the rows, taken cyclically, in which the row in slot s of row i stands s - (13 - 1) // 2 places after row i. With owners the aligned groups of 4 rows, the slots of one owner's rows hold at most 2 rows of any one other owner, and some pair of owners has exactly 2. Over the slots s of one owner's rows that hold rows of one other owner, the sum of 13 - |s - (13 - 1) // 2| is at most 16, and exactly 16 for some pair of owners. block_values[j, 12 - s] is the transpose of block_values[i, s] where slot s of row i holds j; blocks of empty slots are zero.
All inputs are finite; a program needn't handle non-finite values.
Results may differ from a plain program's by a relative error of at most 0.0039.
Values may be sent and summed in bfloat16 or wider, within the bound.
A program may use at most 128 MiB of HBM per device.

v0:
```python
import functools

import jax
import jax.numpy as jnp
from jax import lax
from jax.experimental import pallas as pl
from jax.experimental.pallas import tpu as pltpu
from jax.sharding import PartitionSpec as P

CAP = 2
CHUNKS = 2
BATCHES = 3
MESH = pl.DeviceIdType.MESH


def sends(offset, other):
    if (offset > 0) == (other > 0):
        return abs(other) >= abs(offset)
    return abs(other) < abs(offset) or (abs(other) == abs(offset) and offset > 0)


def kernel(
    owners, rows, slots, size, strip, band, pad, most,
    cl_hbm, blocks_hbm, out,
    cl, blocks, loc, send, tab, win, own, sq, gat, full, turned, pieces, joined, shuffle,
    owner_of, first_code, first_weight, remote_base, local_base, is_local, entries, cum, where_sent, source,
    send_sem, recv_sem, xsend_sem, xrecv_sem, csend_sem, crecv_sem, in_sem,
):
    middle = (slots - 1) // 2
    count = rows * slots
    parts = size // strip
    me = lax.axis_index("rows")
    part = lax.axis_index("cols")
    high, low = part // 2, part % 2
    sibling = high * 2 + (1 - low)
    across = (1 - high) * 2 + low
    far = (1 - high) * 2 + (1 - low)
    partners = (across, sibling, far)
    first = me * rows
    local_at = owners * pad
    turn_at = local_at + count
    chunk = (most - rows * rows) // CHUNKS
    groups = pad // parts
    bounds = [-(-(owners - 1) * q // BATCHES) for q in range(BATCHES + 1)]
    batches = list(zip(bounds[:-1], bounds[1:]))
    early = (owners - 1) // 2
    crossing_at = rows * rows
    part_rows = pl.ds(pl.multiple_of(part * strip, strip), strip)

    def peer_of(j):
        return lax.rem(me + owners // 2 + ((j + 1) // 2) * (1 - 2 * (j % 2)), owners)

    cl_copy = pltpu.make_async_copy(cl_hbm, cl, in_sem.at[0])
    blocks_copy = pltpu.make_async_copy(blocks_hbm, blocks, in_sem.at[1])
    cl_copy.start()
    blocks_copy.start()

    barrier = pltpu.get_barrier_semaphore()

    @pl.loop(0, owners - 1)
    def _(j):
        pl.semaphore_signal(barrier, inc=1, device_id={"rows": peer_of(j)}, device_id_type=MESH)

    for other in partners:
        pl.semaphore_signal(barrier, inc=1, device_id={"cols": other}, device_id_type=MESH)

    zero_block = jnp.zeros((strip, size), jnp.bfloat16)
    loc[count] = zero_block
    sq[count] = zero_block

    @pl.loop(0, owners)
    def _(o):
        for u in range(band, pad):
            tab[o * pad + u] = zero_block

    cl_copy.wait()
    for k in range(rows):
        for b in range(slots):
            column = cl[b, first + k]
            owner_of[k * slots + b] = jnp.where(column >= 0, jnp.maximum(column, 0) // rows, -1)
    blocks_copy.wait()
    for k in range(rows):
        for b in range(slots):
            n = k * slots + b
            value = blocks[k, b, part_rows, :]
            value = jnp.where(cl[b, first + k] >= 0, value, zero_block)
            loc[n] = value
            tab[local_at + n] = value

    def band_copy(src, dst_owner, peer):
        return pltpu.make_async_remote_copy(
            src_ref=send.at[src],
            dst_ref=tab.at[pl.ds(dst_owner * pad, band)],
            send_sem=send_sem.at[src],
            recv_sem=recv_sem.at[dst_owner],
            device_id={"rows": peer},
            device_id_type=MESH,
        )

    def weight(distance, negative):
        return middle + 1 - distance + jnp.minimum(
            distance - jnp.where(negative, 1, 0), middle - distance
        )

    def fill(j):
        peer = peer_of(j)
        lowest = jnp.int32(count)
        highest = jnp.int32(-1)
        for n in range(count):
            hit = owner_of[n] == peer
            lowest = jnp.minimum(lowest, jnp.where(hit, n, count))
            highest = jnp.maximum(highest, jnp.where(hit, n, -1))
        has_one = highest >= 0
        has_two = highest > lowest
        code0 = jnp.where(has_one, lowest, 0)
        code1 = jnp.where(has_two, highest, 0)
        row0, row1 = code0 // slots, code1 // slots
        slot0, slot1 = code0 - row0 * slots, code1 - row1 * slots
        away0, away1 = jnp.abs(slot0 - middle), jnp.abs(slot1 - middle)
        weight0 = jnp.where(has_one, weight(away0, slot0 > middle), 0)
        weight1 = jnp.where(has_two, weight(away1, slot1 > middle), 0)
        sign0 = jnp.where(slot0 > middle, -1, 1)
        sign1 = jnp.where(slot1 > middle, -1, 1)
        for u in range(band):
            in0 = u < weight0
            in1 = u < weight0 + weight1
            step = jnp.where(in0, u, u - weight0)
            away = jnp.where(in0, away0, away1)
            sign = jnp.where(in0, sign0, sign1)
            same = step < middle + 1 - away
            move = jnp.where(same, step, -(step - middle + 2 * away))
            entry = jnp.where(in0, row0, row1) * slots + middle + sign * move
            entry = jnp.where(in1, entry, count)
            send[peer, u] = loc[entry]
        key0 = cl[slot0, first + row0] * slots + slots - 1 - slot0
        key1 = cl[slot1, first + row1] * slots + slots - 1 - slot1
        swap = has_two & (key1 < key0)
        first_code[peer] = jnp.where(swap, code1, code0)
        first_weight[peer] = jnp.where(
            swap, weight(away1, slot1 < middle), weight(away0, slot0 < middle)
        )

    @pl.loop(0, early)
    def _(j):
        fill(j)

    pl.semaphore_wait(barrier, owners - 1 + 3)

    @pl.loop(0, early)
    def _(j):
        band_copy(peer_of(j), me, peer_of(j)).start()

    @pl.loop(early, owners - 1)
    def _(j):
        fill(j)
        band_copy(peer_of(j), me, peer_of(j)).start()

    first_code[me] = 0
    first_weight[me] = 0

    pick = (
        lax.broadcasted_iota(jnp.int32, (strip, size), 1)
        == lax.broadcasted_iota(jnp.int32, (strip, size), 0) + part * strip
    ).astype(jnp.bfloat16)
    for k in range(rows):
        for b in range(slots):
            n = k * slots + b
            block = blocks[k, b]
            block = jnp.where(cl[b, first + k] >= 0, block, jnp.zeros_like(block))
            own[k, :, b * size : (b + 1) * size] = block
            tab[turn_at + local_at + n] = lax.dot_general(
                pick, block, (((1,), (1,)), ((), ())), preferred_element_type=jnp.float32
            ).astype(jnp.bfloat16)

    running = jnp.int32(0)
    for i in range(rows):
        for a in range(slots):
            n = i * slots + a
            column = cl[a, first + i]
            absent = column < 0
            column = jnp.where(absent, first + i, column)
            owner = column // rows
            running = running + jnp.where(owner == me, 0, 1)
            cum[n] = running
            where_sent[n] = jnp.where(
                owner == me,
                i * rows + column - first,
                jnp.minimum(crossing_at + running - 1, most - 1),
            )
            is_local[n] = jnp.where(owner == me, 1, 0)
            remote_base[n] = owner * pad + jnp.where(first_code[owner] == n, 0, first_weight[owner])
            local_base[n] = local_at + (column - first) * slots

    @pl.loop(0, rows)
    def _(i):
        for a in range(slots):
            for s in range(slots):
                if a == middle or s == middle or abs(a - s) > middle:
                    continue
                away_a, away_s = a - middle, s - middle
                direct = sends(away_s, away_a)
                edge, other = (s, a) if direct else (a, s)
                away_e, away_o = (away_s, away_a) if direct else (away_a, away_s)
                if (away_e > 0) == (away_o > 0):
                    u = abs(away_o) - abs(away_e)
                else:
                    u = middle - abs(away_e) + abs(away_o)
                n = i * slots + edge
                entry = jnp.where(
                    is_local[n] == 1, local_base[n] + (other - edge + middle), remote_base[n] + u
                )
                entries[(i * slots + a) * slots + s] = entry + (0 if direct else turn_at)

    for k in range(rows):
        for a in range(slots):
            lanes = slice(a * size, (a + 1) * size)
            for s in range(slots):
                span = slice(s * strip, (s + 1) * strip)
                if abs(a - s) > middle:
                    win[k, span, lanes] = zero_block
                elif a == middle:
                    win[k, span, lanes] = tab[turn_at + local_at + k * slots + s]
                elif s == middle:
                    win[k, span, lanes] = loc[k * slots + a]

    identity = (
        lax.broadcasted_iota(jnp.int32, (size, size), 0)
        == lax.broadcasted_iota(jnp.int32, (size, size), 1)
    ).astype(jnp.bfloat16)
    wide = parts * size
    line = lax.broadcasted_iota(jnp.int32, (wide, wide), 0)
    from_part, from_block, from_row = line // size, (line % size) // strip, line % strip
    shuffle[...] = (
        lax.broadcasted_iota(jnp.int32, (wide, wide), 1)
        == from_block * size + from_part * strip + from_row
    ).astype(jnp.bfloat16)

    def piece_copy(kind, batch, start):
        begin, end = batches[batch]
        span = pl.ds(begin * groups, (end - begin) * groups)
        other = partners[kind]
        return pltpu.make_async_remote_copy(
            src_ref=turned.at[other, span],
            dst_ref=pieces.at[part if start else other, span],
            send_sem=xsend_sem.at[kind, batch],
            recv_sem=xrecv_sem.at[kind, batch],
            device_id={"cols": other},
            device_id_type=MESH,
        )

    for batch, (begin, end) in enumerate(batches):

        @pl.loop(begin, end)
        def _(j):
            peer = peer_of(j)
            band_copy(peer, peer, peer).wait_recv()
            for g in range(groups):
                stack = jnp.concatenate([tab[peer * pad + g * parts + n] for n in range(parts)], 0)
                flipped = lax.dot_general(
                    identity, stack, (((1,), (1,)), ((), ())), preferred_element_type=jnp.float32
                ).astype(jnp.bfloat16)
                for c in range(parts):
                    turned[c, j * groups + g] = flipped[c * strip : (c + 1) * strip]
                pieces[part, j * groups + g] = turned[part, j * groups + g]

        for kind in range(3):
            piece_copy(kind, batch, True).start()

        if batch == 0:
            for i in range(rows):
                for k in range(rows):
                    entry = jnp.int32(count)
                    for a in range(slots):
                        entry = jnp.where(cl[a, first + i] == first + k, i * slots + a, entry)
                    source[i * rows + k] = entry

            @pl.loop(0, most - crossing_at)
            def _(t):
                entry = jnp.int32(0)
                for n in range(count):
                    entry = entry + jnp.where(cum[n] <= t, 1, 0)
                source[crossing_at + t] = entry

    for batch, (begin, end) in enumerate(batches):
        for kind in range(3):
            piece_copy(kind, batch, False).wait_recv()

        for c in range(parts):
            lanes = slice(c * size, (c + 1) * size)
            for g in range(begin * groups, end * groups):
                joined[g * strip : (g + 1) * strip, lanes] = pieces[c, g]
        spread = jnp.dot(
            joined[begin * groups * strip : end * groups * strip, :], shuffle[...],
            preferred_element_type=jnp.float32,
        ).astype(jnp.bfloat16)
        for j in range(begin, end):
            at = turn_at + peer_of(j) * pad
            for g in range(groups):
                top = ((j - begin) * groups + g) * strip
                for n in range(parts):
                    tab[at + g * parts + n] = spread[top : top + strip, n * size : (n + 1) * size]

    spans = [(i * rows, rows) for i in range(rows)]
    spans += [(crossing_at + q * chunk, chunk) for q in range(CHUNKS)]

    def strip_copy(which, piece, peer, sem):
        span = pl.ds(*spans[piece])
        return pltpu.make_async_remote_copy(
            src_ref=gat.at[which, span],
            dst_ref=gat.at[which, span],
            send_sem=csend_sem.at[sem, piece],
            recv_sem=crecv_sem.at[sem, piece],
            device_id={"cols": peer},
            device_id_type=MESH,
        )

    def send_strips(piece):
        begin, length = spans[piece]
        for t in range(begin, begin + length):
            gat[part, t] = sq[source[t]]
        strip_copy(part, piece, across, 0).start()
        strip_copy(part, piece, sibling, 1).start()

    def build(i):
        for a in range(slots):
            for s in range(slots):
                if a == middle or s == middle or abs(a - s) > middle:
                    continue
                win[i, s * strip : (s + 1) * strip, a * size : (a + 1) * size] = tab[
                    entries[(i * slots + a) * slots + s]
                ]

    build(0)
    for i in range(rows):
        if i + 1 < rows:
            build(i + 1)
        total = lax.dot_general(
            win[i], own[i], (((1,), (1,)), ((), ())), preferred_element_type=jnp.float32
        )
        for s in range(slots):
            value = total[s * strip : (s + 1) * strip]
            value = jnp.where(cl[s, first + i] >= 0, value, 0.0)
            sq[i * slots + s] = value.astype(jnp.bfloat16)
        send_strips(i)
    for piece in range(rows, len(spans)):
        send_strips(piece)

    for piece in range(len(spans)):
        strip_copy(across, piece, across, 0).wait_recv()
        strip_copy(across, piece, sibling, 2).start()
    for piece in range(len(spans)):
        strip_copy(sibling, piece, sibling, 1).wait_recv()
    for piece in range(len(spans)):
        strip_copy(far, piece, sibling, 2).wait_recv()

    for i in range(rows):
        for a in range(slots):
            n = i * slots + a
            present = cl[a, first + i] >= 0
            entry = where_sent[n]
            for c in range(parts):
                value = gat[c, entry]
                value = jnp.where(present, value, zero_block)
                full[i, a * size + c * strip : a * size + (c + 1) * strip, :] = value
        total = jnp.dot(win[i], full[i], preferred_element_type=jnp.float32)
        for s in range(slots):
            value = 3.0 * sq[i * slots + s].astype(jnp.float32) - 2.0 * total[s * strip : (s + 1) * strip]
            value = jnp.where(cl[s, first + i] >= 0, value, 0.0)
            out[i, s] = value.astype(jnp.bfloat16)

    @pl.loop(0, owners - 1)
    def _(j):
        peer = peer_of(j)
        band_copy(peer, me, peer).wait_send()

    for batch in range(len(batches)):
        for kind in range(3):
            piece_copy(kind, batch, True).wait_send()

    for piece in range(len(spans)):
        strip_copy(part, piece, across, 0).wait_send()
        strip_copy(part, piece, sibling, 1).wait_send()
        strip_copy(across, piece, sibling, 2).wait_send()


def body(column_lists, block_values):
    rows, slots, size, _ = block_values.shape
    owners = lax.axis_size("rows")
    parts = lax.axis_size("cols")
    assert parts == 4
    strip = size // parts
    middle = (slots - 1) // 2
    band = middle + 1
    pad = -(-band // parts) * parts
    groups = pad // parts
    peers = owners - 1
    count = rows * slots
    crossing = min(count - rows, CAP * peers)
    most = rows * rows + -(-crossing // CHUNKS) * CHUNKS
    bf16 = jnp.bfloat16
    table = 2 * (owners * pad + count)
    result = pl.pallas_call(
        functools.partial(kernel, owners, rows, slots, size, strip, band, pad, most),
        out_shape=jax.ShapeDtypeStruct((rows, slots, strip, size), bf16),
        in_specs=[pl.BlockSpec(memory_space=pl.ANY), pl.BlockSpec(memory_space=pl.ANY)],
        out_specs=pl.BlockSpec(memory_space=pltpu.VMEM),
        scratch_shapes=[
            pltpu.SMEM(column_lists.shape[::-1], jnp.int32),
            pltpu.VMEM(block_values.shape, bf16),
            pltpu.VMEM((count + 1, strip, size), bf16),
            pltpu.VMEM((owners, band, strip, size), bf16),
            pltpu.VMEM((table, strip, size), bf16),
            pltpu.VMEM((rows, slots * strip, slots * size), bf16),
            pltpu.VMEM((rows, size, slots * size), bf16),
            pltpu.VMEM((count + 1, strip, size), bf16),
            pltpu.VMEM((parts, most, strip, size), bf16),
            pltpu.VMEM((rows, slots * size, size), bf16),
            pltpu.VMEM((parts, peers * groups, strip, size), bf16),
            pltpu.VMEM((parts, peers * groups, strip, size), bf16),
            pltpu.VMEM((peers * groups * strip, parts * size), bf16),
            pltpu.VMEM((parts * size, parts * size), bf16),
            pltpu.SMEM((count,), jnp.int32),
            pltpu.SMEM((owners,), jnp.int32),
            pltpu.SMEM((owners,), jnp.int32),
            pltpu.SMEM((count,), jnp.int32),
            pltpu.SMEM((count,), jnp.int32),
            pltpu.SMEM((count,), jnp.int32),
            pltpu.SMEM((count * slots,), jnp.int32),
            pltpu.SMEM((count,), jnp.int32),
            pltpu.SMEM((count,), jnp.int32),
            pltpu.SMEM((most,), jnp.int32),
            pltpu.SemaphoreType.DMA((owners,)),
            pltpu.SemaphoreType.DMA((owners,)),
            pltpu.SemaphoreType.DMA((3, BATCHES)),
            pltpu.SemaphoreType.DMA((3, BATCHES)),
            pltpu.SemaphoreType.DMA((3, rows + CHUNKS)),
            pltpu.SemaphoreType.DMA((3, rows + CHUNKS)),
            pltpu.SemaphoreType.DMA((2,)),
        ],
        compiler_params=pltpu.CompilerParams(
            collective_id=0, has_side_effects=True, vmem_limit_bytes=52 * 1024 * 1024
        ),
    )(column_lists.T, block_values)
    return jnp.swapaxes(result, 2, 3)


def solution(mesh):
    in_specs = (P(), P("rows", None, None, None))
    out_specs = P("rows", None, None, "cols")
    return jax.shard_map(body, mesh=mesh, in_specs=in_specs, out_specs=out_specs, check_vma=False)
```

profile of v0, /device:TPU:1, one launch (start us, length us, event | category | flops | bytes accessed | tf_op | source)
XLA Modules:
  0.0 35.0 jit_solution(14161963292647914377)
XLA Ops:
  0.0 0.0 copy-start
  0.0 0.7 %copy-done = s32[32,13]{0,1:T(8,128)S(1)} copy-done((s32[32,13]{0,1:T(8,128)S(1)}, s32[32,13]{0,1:T(8,128)}, u32[]{:S(2)}) %copy-start) | copy-done | bytes 1688
  0.7 33.6 %shard_map.28 = bf16[4,13,32,128]{3,2,1,0:T(8,128)(2,1)S(1)} custom-call(s32[13,32]{1,0:T(8,128)S(1)} %bitcast.3, bf16[4,13,128,128]{3,2,1,0:T(8,128)(2,1)} %blocks_hbm.1), custom_call_target="tpu_custom_call" | custom-call | tf_op jit(solution)/shard_map/pallas_call | solution.py:402
  34.3 0.8 %copy.4 = bf16[4,13,128,32]{2,3,1,0:T(8,128)(2,1)} copy(bf16[4,13,128,32]{2,3,1,0:T(8,128)(2,1)S(1)} %bitcast.2) | data formatting | bytes 851968
Async XLA Ops:
  0.0 0.7 %copy-start = (s32[32,13]{0,1:T(8,128)S(1)}, s32[32,13]{0,1:T(8,128)}, u32[]{:S(2)}) copy-start(s32[32,13]{0,1:T(8,128)} %param.2) | copy-start | bytes 4996
where the time goes:
time: 35.2 us; the launch traced here: 35 us
  Pallas kernels  33.6 us (95%)
  local copies, waits for them, and re-layouts  1.46 us (4%)
    pallas_call x1, Pallas kernels, body(): pl.pallas_call(functools.partial(kernel, owners, rows, slots, size, strip...  33.6 us
    unnamed x3, local copies, waits for them, and re-layouts  1.46 us

commit v1 on v0

--- a/solution.py
+++ b/solution.py
@@ -41,18 +41,27 @@
     turn_at = local_at + count
     chunk = (most - rows * rows) // CHUNKS
     groups = pad // parts
-    bounds = [-(-(owners - 1) * q // BATCHES) for q in range(BATCHES + 1)]
+    bounds = [0, owners // 2 - 1, (3 * owners) // 4 - 1, owners - 1]
     batches = list(zip(bounds[:-1], bounds[1:]))
     early = (owners - 1) // 2
     crossing_at = rows * rows
     part_rows = pl.ds(pl.multiple_of(part * strip, strip), strip)
 
     def peer_of(j):
-        return lax.rem(me + owners // 2 + ((j + 1) // 2) * (1 - 2 * (j % 2)), owners)
+        peer, bit = 0, 1
+        while bit < owners:
+            peer = peer + ((me // bit + (j + 1) // bit) % 2) * bit
+            bit *= 2
+        return peer
+
+    def in_turn(j):
+        return (j // 2 + owners // 2) * (1 - j % 2) + ((j + 1) // 2) * (j % 2) - 1
 
     cl_copy = pltpu.make_async_copy(cl_hbm, cl, in_sem.at[0])
+    loc_copy = pltpu.make_async_copy(blocks_hbm.at[:, :, part_rows, :], loc, in_sem.at[2])
     blocks_copy = pltpu.make_async_copy(blocks_hbm, blocks, in_sem.at[1])
     cl_copy.start()
+    loc_copy.start()
     blocks_copy.start()
 
     barrier = pltpu.get_barrier_semaphore()
@@ -65,7 +74,6 @@
         pl.semaphore_signal(barrier, inc=1, device_id={"cols": other}, device_id_type=MESH)
 
     zero_block = jnp.zeros((strip, size), jnp.bfloat16)
-    loc[count] = zero_block
     sq[count] = zero_block
 
     @pl.loop(0, owners)
@@ -78,14 +86,7 @@
         for b in range(slots):
             column = cl[b, first + k]
             owner_of[k * slots + b] = jnp.where(column >= 0, jnp.maximum(column, 0) // rows, -1)
-    blocks_copy.wait()
-    for k in range(rows):
-        for b in range(slots):
-            n = k * slots + b
-            value = blocks[k, b, part_rows, :]
-            value = jnp.where(cl[b, first + k] >= 0, value, zero_block)
-            loc[n] = value
-            tab[local_at + n] = value
+    loc_copy.wait()
 
     def band_copy(src, dst_owner, peer):
         return pltpu.make_async_remote_copy(
@@ -102,8 +103,7 @@
             distance - jnp.where(negative, 1, 0), middle - distance
         )
 
-    def fill(j):
-        peer = peer_of(j)
+    def fill(peer):
         lowest = jnp.int32(count)
         highest = jnp.int32(-1)
         for n in range(count):
@@ -129,9 +129,10 @@
             sign = jnp.where(in0, sign0, sign1)
             same = step < middle + 1 - away
             move = jnp.where(same, step, -(step - middle + 2 * away))
-            entry = jnp.where(in0, row0, row1) * slots + middle + sign * move
-            entry = jnp.where(in1, entry, count)
-            send[peer, u] = loc[entry]
+            row = jnp.where(in0, row0, row1)
+            slot = jnp.where(in1, middle + sign * move, middle)
+            used = in1 & (owner_of[row * slots + slot] >= 0)
+            send[peer, u] = jnp.where(used, loc[row, slot], zero_block)
         key0 = cl[slot0, first + row0] * slots + slots - 1 - slot0
         key1 = cl[slot1, first + row1] * slots + slots - 1 - slot1
         swap = has_two & (key1 < key0)
@@ -142,35 +143,42 @@
 
     @pl.loop(0, early)
     def _(j):
-        fill(j)
+        fill(peer_of(in_turn(j)))
 
     pl.semaphore_wait(barrier, owners - 1 + 3)
 
     @pl.loop(0, early)
     def _(j):
-        band_copy(peer_of(j), me, peer_of(j)).start()
+        peer = peer_of(in_turn(j))
+        band_copy(peer, me, peer).start()
 
     @pl.loop(early, owners - 1)
     def _(j):
-        fill(j)
-        band_copy(peer_of(j), me, peer_of(j)).start()
+        peer = peer_of(in_turn(j))
+        fill(peer)
+        band_copy(peer, me, peer).start()
 
     first_code[me] = 0
     first_weight[me] = 0
 
-    pick = (
-        lax.broadcasted_iota(jnp.int32, (strip, size), 1)
-        == lax.broadcasted_iota(jnp.int32, (strip, size), 0) + part * strip
-    ).astype(jnp.bfloat16)
-    for k in range(rows):
+    blocks_copy.wait()
+
+    @pl.loop(0, rows)
+    def _(k):
         for b in range(slots):
             n = k * slots + b
+            present = cl[b, first + k] >= 0
             block = blocks[k, b]
-            block = jnp.where(cl[b, first + k] >= 0, block, jnp.zeros_like(block))
-            own[k, :, b * size : (b + 1) * size] = block
-            tab[turn_at + local_at + n] = lax.dot_general(
-                pick, block, (((1,), (1,)), ((), ())), preferred_element_type=jnp.float32
-            ).astype(jnp.bfloat16)
+            block = jnp.where(present, block, jnp.zeros_like(block))
+            own[k, b * size : (b + 1) * size, :] = block.T
+            value = jnp.where(present, loc[k, b], zero_block)
+            tab[local_at + n] = value
+            if b != middle:
+                win[k, middle * strip : (middle + 1) * strip, b * size : (b + 1) * size] = value
+        for b in range(slots):
+            value = own[k, pl.ds(pl.multiple_of(b * size + part * strip, strip), strip), :]
+            tab[turn_at + local_at + k * slots + b] = value
+            win[k, b * strip : (b + 1) * strip, middle * size : (middle + 1) * size] = value
 
     running = jnp.int32(0)
     for i in range(rows):
@@ -211,22 +219,13 @@
                 )
                 entries[(i * slots + a) * slots + s] = entry + (0 if direct else turn_at)
 
-    for k in range(rows):
+    @pl.loop(0, rows)
+    def _(k):
         for a in range(slots):
-            lanes = slice(a * size, (a + 1) * size)
             for s in range(slots):
-                span = slice(s * strip, (s + 1) * strip)
                 if abs(a - s) > middle:
-                    win[k, span, lanes] = zero_block
-                elif a == middle:
-                    win[k, span, lanes] = tab[turn_at + local_at + k * slots + s]
-                elif s == middle:
-                    win[k, span, lanes] = loc[k * slots + a]
-
-    identity = (
-        lax.broadcasted_iota(jnp.int32, (size, size), 0)
-        == lax.broadcasted_iota(jnp.int32, (size, size), 1)
-    ).astype(jnp.bfloat16)
+                    win[k, s * strip : (s + 1) * strip, a * size : (a + 1) * size] = zero_block
+
     wide = parts * size
     line = lax.broadcasted_iota(jnp.int32, (wide, wide), 0)
     from_part, from_block, from_row = line // size, (line % size) // strip, line % strip
@@ -254,11 +253,13 @@
         def _(j):
             peer = peer_of(j)
             band_copy(peer, peer, peer).wait_recv()
+
+        @pl.loop(begin, end, unroll=min(end - begin, 4))
+        def _(j):
+            peer = peer_of(j)
             for g in range(groups):
                 stack = jnp.concatenate([tab[peer * pad + g * parts + n] for n in range(parts)], 0)
-                flipped = lax.dot_general(
-                    identity, stack, (((1,), (1,)), ((), ())), preferred_element_type=jnp.float32
-                ).astype(jnp.bfloat16)
+                flipped = stack.T
                 for c in range(parts):
                     turned[c, j * groups + g] = flipped[c * strip : (c + 1) * strip]
                 pieces[part, j * groups + g] = turned[part, j * groups + g]
@@ -334,9 +335,7 @@
     for i in range(rows):
         if i + 1 < rows:
             build(i + 1)
-        total = lax.dot_general(
-            win[i], own[i], (((1,), (1,)), ((), ())), preferred_element_type=jnp.float32
-        )
+        total = jnp.dot(win[i], own[i], preferred_element_type=jnp.float32)
         for s in range(slots):
             value = total[s * strip : (s + 1) * strip]
             value = jnp.where(cl[s, first + i] >= 0, value, 0.0)
@@ -407,11 +406,11 @@
         scratch_shapes=[
             pltpu.SMEM(column_lists.shape[::-1], jnp.int32),
             pltpu.VMEM(block_values.shape, bf16),
-            pltpu.VMEM((count + 1, strip, size), bf16),
+            pltpu.VMEM((rows, slots, strip, size), bf16),
             pltpu.VMEM((owners, band, strip, size), bf16),
             pltpu.VMEM((table, strip, size), bf16),
             pltpu.VMEM((rows, slots * strip, slots * size), bf16),
-            pltpu.VMEM((rows, size, slots * size), bf16),
+            pltpu.VMEM((rows, slots * size, size), bf16),
             pltpu.VMEM((count + 1, strip, size), bf16),
             pltpu.VMEM((parts, most, strip, size), bf16),
             pltpu.VMEM((rows, slots * size, size), bf16),
@@ -435,7 +434,7 @@
             pltpu.SemaphoreType.DMA((3, BATCHES)),
             pltpu.SemaphoreType.DMA((3, rows + CHUNKS)),
             pltpu.SemaphoreType.DMA((3, rows + CHUNKS)),
-            pltpu.SemaphoreType.DMA((2,)),
+            pltpu.SemaphoreType.DMA((3,)),
         ],
         compiler_params=pltpu.CompilerParams(
             collective_id=0, has_side_effects=True, vmem_limit_bytes=52 * 1024 * 1024

time: 35.2 us -> 33.1 us (0.940)
  Pallas kernels: 33.6 us -> 31.4 us
    pallas_call x1, Pallas kernels: 33.6 us -> 31.4 us  [body(): pl.pallas_call(functools.partial(kernel, owners, rows, slots, size, strip...]
where the time goes in v1:
time: 33.1 us; the launch traced here: 32.9 us
  Pallas kernels  31.4 us (95%)
  local copies, waits for them, and re-layouts  1.46 us (4%)
    pallas_call x1, Pallas kernels, body(): pl.pallas_call(functools.partial(kernel, owners, rows, slots, size, strip...  31.4 us
    unnamed x3, local copies, waits for them, and re-layouts  1.46 us

profile of v1, /device:TPU:1, one launch (start us, length us, event | category | flops | bytes accessed | tf_op | source)
XLA Modules:
  0.0 32.9 jit_solution(8945793664556627591)
XLA Ops:
  0.0 0.0 copy-start
  0.0 0.7 %copy-done = s32[32,13]{0,1:T(8,128)S(1)} copy-done((s32[32,13]{0,1:T(8,128)S(1)}, s32[32,13]{0,1:T(8,128)}, u32[]{:S(2)}) %copy-start) | copy-done | bytes 1688
  0.7 31.4 %shard_map.28 = bf16[4,13,32,128]{3,2,1,0:T(8,128)(2,1)S(1)} custom-call(s32[13,32]{1,0:T(8,128)S(1)} %bitcast.3, bf16[4,13,128,128]{3,2,1,0:T(8,128)(2,1)} %blocks_hbm.1), custom_call_target="tpu_custom_call" | custom-call | tf_op jit(solution)/shard_map/pallas_call | solution.py:401
  32.1 0.8 %copy.4 = bf16[4,13,128,32]{2,3,1,0:T(8,128)(2,1)} copy(bf16[4,13,128,32]{2,3,1,0:T(8,128)(2,1)S(1)} %bitcast.2) | data formatting | bytes 851968
Async XLA Ops:
  0.0 0.7 %copy-start = (s32[32,13]{0,1:T(8,128)S(1)}, s32[32,13]{0,1:T(8,128)}, u32[]{:S(2)}) copy-start(s32[32,13]{0,1:T(8,128)} %param.2) | copy-start | bytes 4996

commit v2 on v1

--- a/solution.py
+++ b/solution.py
@@ -22,7 +22,7 @@
 def kernel(
     owners, rows, slots, size, strip, band, pad, most,
     cl_hbm, blocks_hbm, out,
-    cl, blocks, loc, send, tab, win, own, sq, gat, full, turned, pieces, joined, shuffle,
+    cl, blocks, loc, send, tab, win, own, sq, near, away, full, halves, partial, turned, pieces, joined, shuffle,
     owner_of, first_code, first_weight, remote_base, local_base, is_local, entries, cum, where_sent, source,
     send_sem, recv_sem, xsend_sem, xrecv_sem, csend_sem, crecv_sem, in_sem,
 ):
@@ -35,7 +35,7 @@
     sibling = high * 2 + (1 - low)
     across = (1 - high) * 2 + low
     far = (1 - high) * 2 + (1 - low)
-    partners = (across, sibling, far)
+    partners = (across, far, sibling)
     first = me * rows
     local_at = owners * pad
     turn_at = local_at + count
@@ -43,7 +43,7 @@
     groups = pad // parts
     bounds = [0, owners // 2 - 1, (3 * owners) // 4 - 1, owners - 1]
     batches = list(zip(bounds[:-1], bounds[1:]))
-    early = (owners - 1) // 2
+    early = 1
     crossing_at = rows * rows
     part_rows = pl.ds(pl.multiple_of(part * strip, strip), strip)
 
@@ -304,23 +304,32 @@
     spans = [(i * rows, rows) for i in range(rows)]
     spans += [(crossing_at + q * chunk, chunk) for q in range(CHUNKS)]
 
-    def strip_copy(which, piece, peer, sem):
+    def strip_copy(src, dst, which, piece, peer, sem):
         span = pl.ds(*spans[piece])
         return pltpu.make_async_remote_copy(
-            src_ref=gat.at[which, span],
-            dst_ref=gat.at[which, span],
+            src_ref=src.at[which, span],
+            dst_ref=dst.at[which, span],
             send_sem=csend_sem.at[sem, piece],
             recv_sem=crecv_sem.at[sem, piece],
             device_id={"cols": peer},
             device_id_type=MESH,
         )
 
+    def to_across(piece):
+        return strip_copy(near, away, low, piece, across, 0)
+
+    def to_sibling(piece, which):
+        return strip_copy(near, near, which, piece, sibling, 1)
+
+    def forward(piece, which):
+        return strip_copy(away, away, which, piece, sibling, 2)
+
     def send_strips(piece):
         begin, length = spans[piece]
         for t in range(begin, begin + length):
-            gat[part, t] = sq[source[t]]
-        strip_copy(part, piece, across, 0).start()
-        strip_copy(part, piece, sibling, 1).start()
+            near[low, t] = sq[source[t]]
+        to_across(piece).start()
+        to_sibling(piece, low).start()
 
     def build(i):
         for a in range(slots):
@@ -344,24 +353,47 @@
     for piece in range(rows, len(spans)):
         send_strips(piece)
 
+    wide_half = size // 2
+    for i in range(rows):
+        for a in range(0, slots, 2):
+            lanes = slice(a * wide_half, a * wide_half + size)
+            left = win[i, :, a * size : (a + 1) * size]
+            if a + 1 < slots:
+                right = win[i, :, (a + 1) * size : (a + 2) * size]
+            else:
+                right = jnp.zeros_like(left)
+            for h in range(2):
+                cut = slice(h * wide_half, (h + 1) * wide_half)
+                halves[h, i, :, lanes] = jnp.concatenate([left[:, cut], right[:, cut]], 1)
+
+    def stack_half(i, strips):
+        for a in range(slots + slots % 2):
+            top = a * wide_half
+            for c in range(2):
+                if a < slots:
+                    value = strips[c, where_sent[i * slots + a]]
+                    value = jnp.where(cl[a, first + i] >= 0, value, zero_block)
+                else:
+                    value = zero_block
+                full[i, top + c * strip : top + (c + 1) * strip, :] = value
+
     for piece in range(len(spans)):
-        strip_copy(across, piece, across, 0).wait_recv()
-        strip_copy(across, piece, sibling, 2).start()
+        to_sibling(piece, 1 - low).wait_recv()
+    for i in range(rows):
+        stack_half(i, near)
+        partial[i] = jnp.dot(halves[high, i], full[i], preferred_element_type=jnp.float32)
+
     for piece in range(len(spans)):
-        strip_copy(sibling, piece, sibling, 1).wait_recv()
+        to_across(piece).wait_recv()
+        forward(piece, low).start()
     for piece in range(len(spans)):
-        strip_copy(far, piece, sibling, 2).wait_recv()
+        forward(piece, 1 - low).wait_recv()
 
     for i in range(rows):
-        for a in range(slots):
-            n = i * slots + a
-            present = cl[a, first + i] >= 0
-            entry = where_sent[n]
-            for c in range(parts):
-                value = gat[c, entry]
-                value = jnp.where(present, value, zero_block)
-                full[i, a * size + c * strip : a * size + (c + 1) * strip, :] = value
-        total = jnp.dot(win[i], full[i], preferred_element_type=jnp.float32)
+        stack_half(i, away)
+        total = partial[i] + jnp.dot(
+            halves[1 - high, i], full[i], preferred_element_type=jnp.float32
+        )
         for s in range(slots):
             value = 3.0 * sq[i * slots + s].astype(jnp.float32) - 2.0 * total[s * strip : (s + 1) * strip]
             value = jnp.where(cl[s, first + i] >= 0, value, 0.0)
@@ -377,9 +409,9 @@
             piece_copy(kind, batch, True).wait_send()
 
     for piece in range(len(spans)):
-        strip_copy(part, piece, across, 0).wait_send()
-        strip_copy(part, piece, sibling, 1).wait_send()
-        strip_copy(across, piece, sibling, 2).wait_send()
+        to_across(piece).wait_send()
+        to_sibling(piece, low).wait_send()
+        forward(piece, low).wait_send()
 
 
 def body(column_lists, block_values):
@@ -393,6 +425,7 @@
     pad = -(-band // parts) * parts
     groups = pad // parts
     peers = owners - 1
+    half_sum = (slots + slots % 2) * size // 2
     count = rows * slots
     crossing = min(count - rows, CAP * peers)
     most = rows * rows + -(-crossing // CHUNKS) * CHUNKS
@@ -412,8 +445,11 @@
             pltpu.VMEM((rows, slots * strip, slots * size), bf16),
             pltpu.VMEM((rows, slots * size, size), bf16),
             pltpu.VMEM((count + 1, strip, size), bf16),
-            pltpu.VMEM((parts, most, strip, size), bf16),
-            pltpu.VMEM((rows, slots * size, size), bf16),
+            pltpu.VMEM((2, most, strip, size), bf16),
+            pltpu.VMEM((2, most, strip, size), bf16),
+            pltpu.VMEM((rows, half_sum, size), bf16),
+            pltpu.VMEM((2, rows, slots * strip, half_sum), bf16),
+            pltpu.VMEM((rows, slots * strip, size), jnp.float32),
             pltpu.VMEM((parts, peers * groups, strip, size), bf16),
             pltpu.VMEM((parts, peers * groups, strip, size), bf16),
             pltpu.VMEM((peers * groups * strip, parts * size), bf16),

time: 33.1 us -> 32.6 us (0.985)
  Pallas kernels: 31.4 us -> 30.7 us
    pallas_call x1, Pallas kernels: 31.4 us -> 30.7 us  [body(): pl.pallas_call(functools.partial(kernel, owners, rows, slots, size, strip...]
where the time goes in v2:
time: 32.6 us; the launch traced here: 32.2 us
  Pallas kernels  30.7 us (94%)
  local copies, waits for them, and re-layouts  1.46 us (4%)
    pallas_call x1, Pallas kernels, body(): pl.pallas_call(functools.partial(kernel, owners, rows, slots, size, strip...  30.7 us
    unnamed x3, local copies, waits for them, and re-layouts  1.46 us

profile of v2, /device:TPU:1, one launch (start us, length us, event | category | flops | bytes accessed | tf_op | source)
XLA Modules:
  0.0 32.2 jit_solution(9343891283896225337)
XLA Ops:
  0.0 0.0 copy-start
  0.0 0.7 %copy-done = s32[32,13]{0,1:T(8,128)S(1)} copy-done((s32[32,13]{0,1:T(8,128)S(1)}, s32[32,13]{0,1:T(8,128)}, u32[]{:S(2)}) %copy-start) | copy-done | bytes 1688
  0.7 30.7 %shard_map.28 = bf16[4,13,32,128]{3,2,1,0:T(8,128)(2,1)S(1)} custom-call(s32[13,32]{1,0:T(8,128)S(1)} %bitcast.3, bf16[4,13,128,128]{3,2,1,0:T(8,128)(2,1)} %blocks_hbm.1), custom_call_target="tpu_custom_call" | custom-call | tf_op jit(solution)/shard_map/pallas_call | solution.py:434
  31.4 0.8 %copy.4 = bf16[4,13,128,32]{2,3,1,0:T(8,128)(2,1)} copy(bf16[4,13,128,32]{2,3,1,0:T(8,128)(2,1)S(1)} %bitcast.2) | data formatting | bytes 851968
Async XLA Ops:
  0.0 0.7 %copy-start = (s32[32,13]{0,1:T(8,128)S(1)}, s32[32,13]{0,1:T(8,128)}, u32[]{:S(2)}) copy-start(s32[32,13]{0,1:T(8,128)} %param.2) | copy-start | bytes 4996

commit v3 on v2

--- a/solution.py
+++ b/solution.py
@@ -9,7 +9,7 @@
 
 CAP = 2
 CHUNKS = 2
-BATCHES = 3
+BATCHES = 4
 MESH = pl.DeviceIdType.MESH
 
 
@@ -41,7 +41,7 @@
     turn_at = local_at + count
     chunk = (most - rows * rows) // CHUNKS
     groups = pad // parts
-    bounds = [0, owners // 2 - 1, (3 * owners) // 4 - 1, owners - 1]
+    bounds = [0, owners // 2 - 1, 3 * owners // 4 - 1, 7 * owners // 8 - 1, owners - 1]
     batches = list(zip(bounds[:-1], bounds[1:]))
     early = 1
     crossing_at = rows * rows

time: 32.6 us -> 32.8 us (level)
  the two profiles are of different devices: /device:TPU:1 before, /device:TPU:7 now
where the time goes in v3:
time: 32.8 us; the launch traced here: 32.6 us
  Pallas kernels  31.2 us (95%)
  local copies, waits for them, and re-layouts  1.46 us (4%)
    pallas_call x1, Pallas kernels, body(): pl.pallas_call(functools.partial(kernel, owners, rows, slots, size, strip...  31.2 us
    unnamed x3, local copies, waits for them, and re-layouts  1.46 us

profile of v3, /device:TPU:7, one launch (start us, length us, event | category | flops | bytes accessed | tf_op | source)
XLA Modules:
  0.0 32.6 jit_solution(309628530179878626)
XLA Ops:
  0.0 0.0 copy-start
  0.0 0.7 %copy-done = s32[32,13]{0,1:T(8,128)S(1)} copy-done((s32[32,13]{0,1:T(8,128)S(1)}, s32[32,13]{0,1:T(8,128)}, u32[]{:S(2)}) %copy-start) | copy-done | bytes 1688
  0.7 31.2 %shard_map.28 = bf16[4,13,32,128]{3,2,1,0:T(8,128)(2,1)S(1)} custom-call(s32[13,32]{1,0:T(8,128)S(1)} %bitcast.3, bf16[4,13,128,128]{3,2,1,0:T(8,128)(2,1)} %blocks_hbm.1), custom_call_target="tpu_custom_call" | custom-call | tf_op jit(solution)/shard_map/pallas_call | solution.py:434
  31.9 0.8 %copy.4 = bf16[4,13,128,32]{2,3,1,0:T(8,128)(2,1)} copy(bf16[4,13,128,32]{2,3,1,0:T(8,128)(2,1)S(1)} %bitcast.2) | data formatting | bytes 851968
Async XLA Ops:
  0.0 0.7 %copy-start = (s32[32,13]{0,1:T(8,128)S(1)}, s32[32,13]{0,1:T(8,128)}, u32[]{:S(2)}) copy-start(s32[32,13]{0,1:T(8,128)} %param.2) | copy-start | bytes 4996
